TPU v7x, 32 devices: a whole 2x2x4 slice. The times are simulated.
32 devices in a mesh: groups: 2 (over x), seq: 16 (over z, y, core).
Axes of the slice: x: 2, y: 2, z: 4, core: 2. Of those that a mesh axis runs over, the one named last changes fastest.
Arguments:
- latent_noise: float32 [4096, 192], P(('groups', 'seq')), parts along dimension 0, may hold values from -6 to 6
- position: bfloat16 [2048, 768], P('seq'), may hold values from -2 to 2
- in_weight: bfloat16 [192, 768], replicated, may hold values from -0.4375 to 0.4375
- gain_attn: float32 [768], replicated, may hold values from 0.1 to 1.9
- query_weight: bfloat16 [768, 384], replicated, may hold values from -5.1 to 5.1
- key_weight: bfloat16 [768, 384], replicated, may hold values from -5.1 to 5.1
- value_weight: bfloat16 [768, 384], replicated, may hold values from -0.21875 to 0.21875
- mix_weight: bfloat16 [384, 768], replicated, may hold values from -0.3125 to 0.3125
- gain_mlp: float32 [768], replicated, may hold values from 0.1 to 1.9
- up_weight: bfloat16 [768, 1536], replicated, may hold values from -0.21875 to 0.21875
- down_weight: bfloat16 [1536, 768], replicated, may hold values from -0.15625 to 0.15625
- gain_out: float32 [768], replicated, may hold values from 0.1 to 1.9
- out_weight: bfloat16 [768, 384], replicated, may hold values from -0.15625 to 0.15625
Outputs:
- sample: float32 [4096, 192], P(('groups', 'seq')), parts along dimension 0
There are 2 independent parts, one for each index of `groups`. A program takes and returns all parts, laid end to end along the dimension named above; an argument that names none is the same for every part. Nothing has to cross between parts.
All inputs are finite; a program needn't handle non-finite values.
Results may differ from a plain program's by a relative error of at most 0.04.
Values may be sent and summed in bfloat16 or wider, within the bound.
A program may use at most 128 MiB of HBM per device.

v0:
```python
import jax
import jax.numpy as jnp
from jax import lax
from jax.sharding import PartitionSpec as P

HEADS = 6
ITERS = 2


def shifted_2(value, axis, steps):
    count = lax.axis_size(axis)
    leading, last = (max(0, -steps), min(count, count - steps))
    return lax.ppermute(value, axis, [(source, source + steps) for source in range(leading, last)])


def swapped(value, axis, distance):
    mask = 2**distance
    pairs = [(source, source ^ mask) for source in range(lax.axis_size(axis))]
    return lax.ppermute(value, axis, pairs)


def rms_norm(values, gain):
    scale = lax.rsqrt(jnp.mean(values * values, axis=-1, keepdims=True) + 1e-06)
    return values * scale * gain


def attend_rows(query_rows, key_rows, value_rows, own_index):
    local_rows = query_rows.shape[0]
    head_dim = query_rows.shape[1] // HEADS
    scale = head_dim ** (-0.5)
    query_heads = query_rows.reshape(local_rows, HEADS, head_dim)
    query_pos = own_index * local_rows + lax.iota(jnp.int32, local_rows)
    old_max = jnp.full((HEADS, local_rows), -1e30, jnp.float32)
    key_piece = lax.all_gather(key_rows, "seq", axis=0, tiled=True)
    value_piece = lax.all_gather(value_rows, "seq", axis=0, tiled=True)
    piece_rows = key_piece.shape[0]
    key_heads = key_piece.reshape(piece_rows, HEADS, head_dim)
    scores = (
        jnp.einsum("qhd,khd->hqk", query_heads, key_heads, preferred_element_type=jnp.float32)
        * scale
    )
    key_pos = lax.iota(jnp.int32, piece_rows)
    causal = (key_pos[None, :] <= query_pos[:, None])[None]
    piece_max = jnp.max(jnp.where(causal, scores, -1e30), axis=2)
    new_max = jnp.maximum(old_max, piece_max)
    weights = jnp.where(causal, jnp.exp(scores - new_max[:, :, None]), 0.0)
    new_total = jnp.sum(weights, axis=2)
    value_heads = value_piece.reshape(piece_rows, HEADS, head_dim)
    product = jnp.einsum(
        "hqk,khd->hqd",
        weights.astype(jnp.bfloat16),
        value_heads,
        preferred_element_type=jnp.float32,
    )
    accumulated = product
    final_max, final_total, accumulated = (new_max, new_total, accumulated)
    result = accumulated / final_total[:, :, None]
    return (
        jnp.transpose(result, (1, 0, 2)).reshape(local_rows, HEADS * head_dim).astype(jnp.bfloat16)
    )


def jacobi_step(
    current,
    latent_noise,
    position,
    in_weight,
    gain_attn,
    query_weight,
    key_weight,
    value_weight,
    mix_weight,
    gain_mlp,
    up_weight,
    down_weight,
    gain_out,
    out_weight,
    own_index,
):
    patch_width = current.shape[1]
    previous = shifted_2(current[-1:], "seq", 1)
    shifted = jnp.concatenate([previous, current[:-1]], axis=0)
    hidden_in = jnp.dot(
        shifted.astype(jnp.bfloat16), in_weight, preferred_element_type=jnp.float32
    ) + position.astype(jnp.float32)
    normed_attn = rms_norm(hidden_in, gain_attn).astype(jnp.bfloat16)
    query_rows = jnp.dot(normed_attn, query_weight, preferred_element_type=jnp.float32).astype(
        jnp.bfloat16
    )
    key_rows = jnp.dot(normed_attn, key_weight, preferred_element_type=jnp.float32).astype(
        jnp.bfloat16
    )
    value_rows = jnp.dot(normed_attn, value_weight, preferred_element_type=jnp.float32).astype(
        jnp.bfloat16
    )
    attended = attend_rows(query_rows, key_rows, value_rows, own_index)
    hidden_mid = hidden_in + jnp.dot(attended, mix_weight, preferred_element_type=jnp.float32)
    normed_mlp = rms_norm(hidden_mid, gain_mlp).astype(jnp.bfloat16)
    activated = jax.nn.gelu(
        jnp.dot(normed_mlp, up_weight, preferred_element_type=jnp.float32)
    ).astype(jnp.bfloat16)
    hidden_out = hidden_mid + jnp.dot(activated, down_weight, preferred_element_type=jnp.float32)
    normed_out = rms_norm(hidden_out, gain_out).astype(jnp.bfloat16)
    statistics = jnp.dot(normed_out, out_weight, preferred_element_type=jnp.float32)
    mean_shift = statistics[:, :patch_width]
    log_scale = statistics[:, patch_width:]
    return latent_noise * jnp.exp(log_scale) + mean_shift


def per_device(
    latent_noise,
    position,
    in_weight,
    gain_attn,
    query_weight,
    key_weight,
    value_weight,
    mix_weight,
    gain_mlp,
    up_weight,
    down_weight,
    gain_out,
    out_weight,
):
    own_index = lax.axis_index("seq")
    current = latent_noise
    for iteration in range(ITERS):
        current = jacobi_step(
            current,
            latent_noise,
            position,
            in_weight,
            gain_attn,
            query_weight,
            key_weight,
            value_weight,
            mix_weight,
            gain_mlp,
            up_weight,
            down_weight,
            gain_out,
            out_weight,
            own_index,
        )
    flipped = current[::-1]
    bit_count = lax.axis_size("seq").bit_length() - 1
    for bit_index in range(bit_count):
        flipped = swapped(flipped, "seq", bit_index)
    return flipped


def solution(mesh):
    in_specs = (
        P(("groups", "seq"), None),
        P("seq", None),
        P(),
        P(),
        P(),
        P(),
        P(),
        P(),
        P(),
        P(),
        P(),
        P(),
        P(),
    )
    out_specs = P(("groups", "seq"), None)
    return jax.shard_map(
        per_device, mesh=mesh, in_specs=in_specs, out_specs=out_specs, check_vma=False
    )
```

profile of v0, /device:TPU:1, one launch (start us, length us, event | category | flops | bytes accessed | tf_op | source)
XLA Modules:
  0.0 240.5 jit_solution(17425421186968204289)
XLA Ops:
  6.5 1.1 slice.26
  7.7 4.5 %collective-permute-start = (bf16[1,192]{0,1:T(8,128)(2,1)S(1)}, bf16[1,192]{0,1:T(8,128)(2,1)S(1)}, u32[]{:S(2)}, u32[]{:S(2)}) collective-permute-start(bf16[1,192]{0,1:T(8,128)(2,1)S(1)} %slice.26), channel_id=1, source_target_pairs={{0,1},{1,2},{2,3},{3,4},{4,5},{5,6},{6,7},{7,8},{8,9},{9,10},{10,1... | collective-permute-start | bytes 1160 | tf_op jit(solution)/shard_map/ppermute | solution.py:13
  12.2 0.9 slice.56
  13.1 0.3 collective-permute-done
  13.4 1.4 multiply_reduce_fusion.5
  14.8 0.8 multiply_convert_fusion.5
  15.6 2.0 convolution_convert_fusion.4
  17.6 0.0 all-gather.5.cloned.1.call-update
  17.6 0.0 all-gather.7.cloned.1.call-start
  17.6 2.0 convolution_convert_fusion.3
  19.6 0.0 all-gather.7.cloned.1.call-update
  19.6 0.0 all-gather.9.cloned.1.call-start
  19.7 1.0 copy.30
  20.7 0.2 iota_compare_fusion
  20.9 1.3 convolution_convert_fusion.5
  22.3 0.1 copy.23
  22.4 37.2 %all-gather.5.cloned.1.call-done = bf16[2048,384]{1,0:T(8,128)(2,1)} async-done(((bf16[128,384]{1,0:T(8,128)(2,1)}), bf16[2048,384]{1,0:T(8,128)(2,1)}) %all-gather.5.cloned.1.call-update) | async-done | bytes 1572880 | tf_op jit(solution)/shard_map/all_gather | solution.py:34
  59.6 2.7 %copy.24 = bf16[2048,384]{0,1:T(8,128)(2,1)} copy(bf16[2048,384]{1,0:T(8,128)(2,1)} %all-gather.5.cloned.1.call-done) | data formatting | bytes 3145728 | tf_op jit(solution)/shard_map/all_gather | solution.py:34
  62.3 2.7 %select_reduce_fusion.1 = (f32[6,128]{1,0:T(8,128)S(1)}, f32[6,128,2048]{2,1,0:T(8,128)S(1)}) fusion(pred[128,2048]{1,0:T(8,128)(4,1)S(1)} %iota_compare_fusion, bf16[128,6,64]{0,2,1:T(8,128)(2,1)S(1)} %bitcast.57, bf16[2048,6,64]{0,2,1:T(8,128)(2,1)} %bitcast.53), kind=kOutput, calls=%fused_computation.3 | convolution fusion | flops 206044416 | bytes 8227840 | tf_op jit(solution)/shard_map/qhd,khd->hqk/dot_general | solution.py:39
  65.1 2.6 %copy-done.2 = f32[6,128,2048]{2,1,0:T(8,128)} copy-done((f32[6,128,2048]{2,1,0:T(8,128)}, f32[6,128,2048]{2,1,0:T(8,128)S(1)}, u32[]{:S(2)}) %copy-start.2) | copy-done | bytes 6291480
  67.7 1.6 fusion
  69.3 31.2 %all-gather.7.cloned.1.call-done = bf16[2048,384]{1,0:T(8,128)(2,1)} async-done(((bf16[128,384]{1,0:T(8,128)(2,1)}), bf16[2048,384]{1,0:T(8,128)(2,1)}) %all-gather.7.cloned.1.call-update) | async-done | bytes 1572880 | tf_op jit(solution)/shard_map/all_gather | solution.py:35
  100.5 2.6 %copy.25 = bf16[2048,384]{0,1:T(8,128)(2,1)} copy(bf16[2048,384]{1,0:T(8,128)(2,1)} %all-gather.7.cloned.1.call-done) | data formatting | bytes 3145728 | tf_op jit(solution)/shard_map/all_gather | solution.py:35
  103.2 4.7 %fusion.25 = bf16[128,6,64]{0,2,1:T(8,128)(2,1)S(1)} fusion(bf16[2048,6,64]{0,2,1:T(8,128)(2,1)} %bitcast.56, f32[6,128,2048]{2,1,0:T(8,128)} %copy-done.2, f32[6,128]{1,0:T(8,128)S(1)} %broadcast_maximum_fusion.1, pred[128,2048]{1,0:T(8,128)(4,1)S(1)} %iota_compare_fusion, f32[128,6]{0,1:T(8,128)S(1)} %bitcast.63), kind=kOutput, calls=%fused_computation.31 | convolution fusion | flops 207716352 | bytes 8230912 | tf_op jit(solution)/shard_map/hqk,khd->hqd/dot_general | solution.py:49
  107.9 0.0 copy-start.7
  107.9 0.0 copy-start.5
  107.9 0.0 copy-start.6
  107.9 1.0 multiply_reduce_fusion.4
  109.0 3.6 %multiply_reduce_fusion.3 = (f32[128]{0:T(128)S(1)}, f32[128,768]{1,0:T(8,128)}) fusion(f32[128,768]{1,0:T(8,128)} %get-tuple-element.10, bf16[1536,768]{1,0:T(8,128)(2,1)S(1)} %copy-done, bf16[768,1536]{1,0:T(8,128)(2,1)} %param.22, f32[768]{0:T(1024)S(1)} %copy-done.8, f32[128]{0:T(128)S(1)} %add_rsqrt_fusion.4), kind=kOutput, calls=%fused_computation.56 | convolution fusion | flops 606338944 | bytes 5509120 | tf_op jit(solution)/shard_map/dot_general | solution.py:102
  112.6 1.5 fusion.55
  114.1 0.1 slice_add_fusion.1
  114.2 2.4 collective-permute-start.1
  116.6 0.7 collective-permute-done.1
  117.3 1.3 multiply_reduce_fusion.2
  118.6 0.1 multiply_convert_fusion.2
  118.7 2.0 convolution_convert_fusion.1
  120.7 0.0 all-gather.9.cloned.1.call-update
  120.7 0.2 all-gather.11.cloned.1.call-start
  120.9 2.0 convolution_convert_fusion
  122.9 0.0 all-gather.11.cloned.1.call-update
  122.9 1.3 convolution_convert_fusion.2
  124.3 0.1 copy.27
  124.4 37.7 %all-gather.9.cloned.1.call-done = bf16[2048,384]{1,0:T(8,128)(2,1)} async-done(((bf16[128,384]{1,0:T(8,128)(2,1)}), bf16[2048,384]{1,0:T(8,128)(2,1)}) %all-gather.9.cloned.1.call-update) | async-done | bytes 1572880 | tf_op jit(solution)/shard_map/all_gather | solution.py:34
  162.1 2.7 %copy.28 = bf16[2048,384]{0,1:T(8,128)(2,1)} copy(bf16[2048,384]{1,0:T(8,128)(2,1)} %all-gather.9.cloned.1.call-done) | data formatting | bytes 3145728 | tf_op jit(solution)/shard_map/all_gather | solution.py:34
  164.8 2.7 %select_reduce_fusion = (f32[6,128]{1,0:T(8,128)S(1)}, f32[6,128,2048]{2,1,0:T(8,128)S(1)}) fusion(pred[128,2048]{1,0:T(8,128)(4,1)S(1)} %iota_compare_fusion, bf16[128,6,64]{0,2,1:T(8,128)(2,1)S(1)} %bitcast.58, bf16[2048,6,64]{0,2,1:T(8,128)(2,1)} %bitcast.54), kind=kOutput, calls=%fused_computation.1 | convolution fusion | flops 206044416 | bytes 8227840 | tf_op jit(solution)/shard_map/qhd,khd->hqk/dot_general | solution.py:39
  167.5 2.6 %copy-done.1 = f32[6,128,2048]{2,1,0:T(8,128)} copy-done((f32[6,128,2048]{2,1,0:T(8,128)}, f32[6,128,2048]{2,1,0:T(8,128)S(1)}, u32[]{:S(2)}) %copy-start.1) | copy-done | bytes 6291480
  170.2 1.6 fusion.2
  171.8 31.1 %all-gather.11.cloned.1.call-done = bf16[2048,384]{1,0:T(8,128)(2,1)} async-done(((bf16[128,384]{1,0:T(8,128)(2,1)}), bf16[2048,384]{1,0:T(8,128)(2,1)}) %all-gather.11.cloned.1.call-update) | async-done | bytes 1572880 | tf_op jit(solution)/shard_map/all_gather | solution.py:35
  202.8 2.6 %copy.29 = bf16[2048,384]{0,1:T(8,128)(2,1)} copy(bf16[2048,384]{1,0:T(8,128)(2,1)} %all-gather.11.cloned.1.call-done) | data formatting | bytes 3145728 | tf_op jit(solution)/shard_map/all_gather | solution.py:35
  205.5 4.7 %fusion.19 = bf16[128,6,64]{0,2,1:T(8,128)(2,1)S(1)} fusion(bf16[2048,6,64]{0,2,1:T(8,128)(2,1)} %bitcast.55, f32[6,128,2048]{2,1,0:T(8,128)} %copy-done.1, f32[6,128]{1,0:T(8,128)S(1)} %broadcast_maximum_fusion, pred[128,2048]{1,0:T(8,128)(4,1)S(1)} %iota_compare_fusion, f32[128,6]{0,1:T(8,128)S(1)} %bitcast.62), kind=kOutput, calls=%fused_computation.29 | convolution fusion | flops 207716352 | bytes 8230912 | tf_op jit(solution)/shard_map/hqk,khd->hqd/dot_general | solution.py:49
  210.2 1.0 multiply_reduce_fusion.1
  211.3 2.9 %multiply_reduce_fusion = (f32[128]{0:T(128)S(1)}, f32[128,768]{1,0:T(8,128)S(1)}) fusion(f32[128,768]{1,0:T(8,128)} %get-tuple-element.18, bf16[1536,768]{1,0:T(8,128)(2,1)S(1)} %copy-done, bf16[768,1536]{1,0:T(8,128)(2,1)} %param.22, f32[128]{0:T(128)S(1)} %add_rsqrt_fusion.1, f32[768]{0:T(1024)S(1)} %copy-done.8), kind=kOutput, calls=%fused_computation.50 | convolution fusion | flops 606338944 | bytes 5509120 | tf_op jit(solution)/shard_map/dot_general | solution.py:102
  214.2 1.4 fusion.57
  215.6 0.1 slice_add_fusion
  215.7 0.1 rev.3
  215.8 0.3 collective-permute-start.2
  216.1 1.1 collective-permute-done.2
  217.2 0.3 collective-permute-start.3
  217.5 4.5 %collective-permute-done.3 = f32[128,192]{1,0:T(8,128)S(1)} collective-permute-done((f32[128,192]{1,0:T(8,128)S(1)}, f32[128,192]{1,0:T(8,128)S(1)}, u32[]{:S(2)}, u32[]{:S(2)}) %collective-permute-start.3) | collective-permute-done | bytes 98336 | tf_op jit(solution)/shard_map/ppermute | solution.py:19
  222.1 0.1 collective-permute-start.4
  222.2 3.7 %collective-permute-done.4 = f32[128,192]{1,0:T(8,128)S(1)} collective-permute-done((f32[128,192]{1,0:T(8,128)S(1)}, f32[128,192]{1,0:T(8,128)S(1)}, u32[]{:S(2)}, u32[]{:S(2)}) %collective-permute-start.4) | collective-permute-done | bytes 98336 | tf_op jit(solution)/shard_map/ppermute | solution.py:19
  225.9 1.2 collective-permute-start.5
  227.0 6.2 %collective-permute-done.5 = f32[128,192]{1,0:T(8,128)S(1)} collective-permute-done((f32[128,192]{1,0:T(8,128)S(1)}, f32[128,192]{1,0:T(8,128)S(1)}, u32[]{:S(2)}, u32[]{:S(2)}) %collective-permute-start.5) | collective-permute-done | bytes 98336 | tf_op jit(solution)/shard_map/ppermute | solution.py:19
  233.3 0.7 copy.31
  (24 shorter events, 0.1 us)
Async XLA Ops:
  6.5 102.4 %copy-start = (bf16[1536,768]{1,0:T(8,128)(2,1)S(1)}, bf16[1536,768]{1,0:T(8,128)(2,1)}, u32[]{:S(2)}) copy-start(bf16[1536,768]{1,0:T(8,128)(2,1)} %param.23) | copy-start | bytes 7077892
  6.5 53.1 %all-gather.5.cloned.1.call-start = ((), (), s32[]{:S(2)}) async-start(), calls=%async_computation | async-start | bytes 1671168 | tf_op jit(solution)/shard_map/all_gather | solution.py:34
  7.7 5.7 %collective-permute-start = (bf16[1,192]{0,1:T(8,128)(2,1)S(1)}, bf16[1,192]{0,1:T(8,128)(2,1)S(1)}, u32[]{:S(2)}, u32[]{:S(2)}) collective-permute-start(bf16[1,192]{0,1:T(8,128)(2,1)S(1)} %slice.26), channel_id=1, source_target_pairs={{0,1},{1,2},{2,3},{3,4},{4,5},{5,6},{6,7},{7,8},{8,9},{9,10},{10,1... | collective-permute-start | bytes 1160 | tf_op jit(solution)/shard_map/ppermute | solution.py:13
  17.6 82.9 %all-gather.7.cloned.1.call-start = ((), (), s32[]{:S(2)}) async-start(), calls=%async_computation.1 | async-start | bytes 1671168 | tf_op jit(solution)/shard_map/all_gather | solution.py:35
  19.6 142.5 %all-gather.9.cloned.1.call-start = ((), (), s32[]{:S(2)}) async-start(), calls=%async_computation.2 | async-start | bytes 1671168 | tf_op jit(solution)/shard_map/all_gather | solution.py:34
  65.0 2.7 %copy-start.2 = (f32[6,128,2048]{2,1,0:T(8,128)}, f32[6,128,2048]{2,1,0:T(8,128)S(1)}, u32[]{:S(2)}) copy-start(f32[6,128,2048]{2,1,0:T(8,128)S(1)} %get-tuple-element.8) | copy-start | bytes 18874372
  103.1 4.8 %copy-start.3 = (bf16[384,768]{1,0:T(8,128)(2,1)S(1)}, bf16[384,768]{1,0:T(8,128)(2,1)}, u32[]{:S(2)}) copy-start(bf16[384,768]{1,0:T(8,128)(2,1)} %param.20) | copy-start | bytes 1769476
  103.2 5.8 %copy-start.8 = (f32[768]{0:T(1024)S(1)}, f32[768]{0:T(1024)}, u32[]{:S(2)}) copy-start(f32[768]{0:T(1024)} %param.21) | copy-start | bytes 9220
  107.9 4.7 %copy-start.7 = (f32[768]{0:T(1024)S(1)}, f32[768]{0:T(1024)}, u32[]{:S(2)}) copy-start(f32[768]{0:T(1024)} %param.24) | copy-start | bytes 9220
  107.9 9.4 %copy-start.5 = (bf16[128,768]{1,0:T(8,128)(2,1)S(1)}, bf16[128,768]{1,0:T(8,128)(2,1)}, u32[]{:S(2)}) copy-start(bf16[128,768]{1,0:T(8,128)(2,1)} %param.14) | copy-start | bytes 589828
  107.9 10.7 %copy-start.6 = (f32[768]{0:T(1024)S(1)}, f32[768]{0:T(1024)}, u32[]{:S(2)}) copy-start(f32[768]{0:T(1024)} %param.16) | copy-start | bytes 9220
  114.2 3.1 %collective-permute-start.1 = (bf16[1,192]{1,0:T(2,128)(2,1)S(1)}, bf16[1,192]{1,0:T(2,128)(2,1)S(1)}, u32[]{:S(2)}, u32[]{:S(2)}) collective-permute-start(bf16[1,192]{1,0:T(2,128)(2,1)S(1)} %slice.37), channel_id=1, source_target_pairs={{0,1},{1,2},{2,3},{3,4},{4,5},{5,6},{6,7},{7,8},{8,9},{9,10},{10,1... | collective-permute-start | bytes 1160 | tf_op jit(solution)/shard_map/ppermute | solution.py:13
  120.7 82.1 %all-gather.11.cloned.1.call-start = ((), (), s32[]{:S(2)}) async-start(), calls=%async_computation.3 | async-start | bytes 1671168 | tf_op jit(solution)/shard_map/all_gather | solution.py:35
  167.5 2.7 %copy-start.1 = (f32[6,128,2048]{2,1,0:T(8,128)}, f32[6,128,2048]{2,1,0:T(8,128)S(1)}, u32[]{:S(2)}) copy-start(f32[6,128,2048]{2,1,0:T(8,128)S(1)} %get-tuple-element.16) | copy-start | bytes 18874372
  205.5 4.7 %copy-start.4 = (bf16[384,768]{1,0:T(8,128)(2,1)S(1)}, bf16[384,768]{1,0:T(8,128)(2,1)}, u32[]{:S(2)}) copy-start(bf16[384,768]{1,0:T(8,128)(2,1)} %param.20) | copy-start | bytes 1769476
  215.8 1.4 collective-permute-start.2
  217.2 4.8 %collective-permute-start.3 = (f32[128,192]{1,0:T(8,128)S(1)}, f32[128,192]{1,0:T(8,128)S(1)}, u32[]{:S(2)}, u32[]{:S(2)}) collective-permute-start(f32[128,192]{1,0:T(8,128)S(1)} %collective-permute-done.2), channel_id=1, source_target_pairs={{0,2},{1,3},{2,0},{3,1},{4,6},{5,7},{6,4},{7,5},{8,10},{9,11},{10,... | collective-permute-start | bytes 294920 | tf_op jit(solution)/shard_map/ppermute | solution.py:19
  222.1 3.8 %collective-permute-start.4 = (f32[128,192]{1,0:T(8,128)S(1)}, f32[128,192]{1,0:T(8,128)S(1)}, u32[]{:S(2)}, u32[]{:S(2)}) collective-permute-start(f32[128,192]{1,0:T(8,128)S(1)} %collective-permute-done.3), channel_id=1, source_target_pairs={{0,4},{1,5},{2,6},{3,7},{4,0},{5,1},{6,2},{7,3},{8,12},{9,13},{10,... | collective-permute-start | bytes 294920 | tf_op jit(solution)/shard_map/ppermute | solution.py:19
  225.9 7.4 %collective-permute-start.5 = (f32[128,192]{1,0:T(8,128)S(1)}, f32[128,192]{1,0:T(8,128)S(1)}, u32[]{:S(2)}, u32[]{:S(2)}) collective-permute-start(f32[128,192]{1,0:T(8,128)S(1)} %collective-permute-done.4), channel_id=1, source_target_pairs={{0,8},{1,9},{2,10},{3,11},{4,12},{5,13},{6,14},{7,15},{8,0},{9,1},... | collective-permute-start | bytes 294920 | tf_op jit(solution)/shard_map/ppermute | solution.py:19
Sparse Core Ops, SparseCore 0:
  17.7 41.8 all-gather.4
  61.9 38.5 all-gather.6
  120.8 41.2 all-gather.8
  164.2 38.5 all-gather.10
where the time goes:
time: 243 us; the launch traced here: 241 us
  waiting for transfers between devices  154 us (63%)
  matrix products  39.6 us (16%)
  local copies, waits for them, and re-layouts  20 us (8%)
  between operations  13.4 us (6%)
  starting transfers between devices  9.17 us (4%)
  other arithmetic  4.6 us (2%)
    all_gather x2, waiting for transfers between devices, attend_rows(): key_piece = lax.all_gather(key_rows, 'seq', axis=0, tiled=True)  75 us
    all_gather x2, waiting for transfers between devices, attend_rows(): value_piece = lax.all_gather(value_rows, 'seq', axis=0, tiled=True)  62.3 us
    ppermute x4, waiting for transfers between devices, swapped(): return lax.ppermute(value, axis, pairs)  15.5 us
    dot_general x2, matrix products, attend_rows(): jnp.einsum('hqk,khd->hqd', weights.astype(jnp.bfloat16), value_heads, pre...  9.45 us
    ppermute x2, starting transfers between devices, shifted_2(): lax.ppermute(value, axis, [(source, source + steps) for source in range(l...  6.91 us
    dot_general x2, matrix products, jacobi_step(): jnp.dot(activated, down_weight, preferred_element_type=jnp.float32)  6.51 us
    unnamed x19, local copies, waits for them, and re-layouts  6.29 us
    dot_general x2, matrix products, attend_rows(): jnp.einsum('qhd,khd->hqk', query_heads, key_heads, preferred_element_type...  5.47 us
  transfers between devices with their start and end apart: 10, of which 10 were waited for; matrix products, arithmetic and copies ran while one was open for 10% of the time, Pallas kernels for 0%

commit v1 on v0

v1 whole, which is shorter than its diff:
```python
import functools

import jax
import jax.numpy as jnp
from jax import lax
from jax.experimental import pallas as pl
from jax.experimental.pallas import tpu as pltpu
from jax.sharding import PartitionSpec as P

HEADS = 6
ITERS = 2
COLS = 4
DOWN, ACROSS, CORE, CORE_FAR = range(4)
TAIL = 16
F32, BF16 = jnp.float32, jnp.bfloat16


def dot(a, b):
    return jnp.dot(a, b, preferred_element_type=F32)


def dot_nt(a, b):
    return lax.dot_general(a, b, (((1,), (1,)), ((), ())), preferred_element_type=F32)


def rms_norm(values, gain):
    scale = lax.rsqrt(jnp.mean(values * values, axis=-1, keepdims=True) + 1e-06)
    return values * scale * gain


def kernel(
    n,
    latent,
    gain_attn,
    gain_mlp,
    gain_out,
    position,
    *refs,
):
    hbm = refs[:8]
    out = refs[8]
    scratch = refs[9:]
    in_w, q_w, k_w, v_w, mix_w, up_w, down_w, out_w = vmem = scratch[:8]
    (
        blocks,
        places,
        tail_src,
        tail_dst,
        queries,
        top,
        total,
        acc,
        current,
        flip_src,
        flip_dst,
        load_sem,
        send_sem,
        recv_sem,
        tail_send,
        tail_recv,
        flip_send,
        flip_recv,
    ) = scratch[8:]
    rows, patch = latent.shape
    width = q_w.shape[1]
    head_dim = width // HEADS
    pair = 2 * head_dim
    pairs = HEADS // 2
    line = n // COLS
    me = lax.axis_index("seq")
    row, col = me // COLS, me % COLS
    across = row * COLS + (col + 2) % COLS
    other = me + 1 - 2 * (me % 2)
    mirror = n - 1 - me

    loads = [
        pltpu.make_async_copy(source, target, load_sem.at[i])
        for i, (source, target) in enumerate(zip(hbm, vmem))
    ]
    own_rows = pl.ds(pl.multiple_of(me * rows, rows), rows)
    place_load = pltpu.make_async_copy(position, places.at[own_rows], load_sem.at[len(loads)])
    place_load.start()
    for load in loads:
        load.start()

    barrier = pltpu.get_barrier_semaphore()

    def greet(device):
        pl.semaphore_signal(barrier, inc=1, device_id={"seq": device}, device_id_type=pl.DeviceIdType.MESH)

    greet(across)
    greet(other)
    greet(mirror)
    pl.when(row > 0)(lambda: greet(me - COLS))
    pl.when(row < line - 1)(lambda: greet(me + COLS))
    pl.when(me > 0)(lambda: greet(me - 1))
    pl.when(me < n - 1)(lambda: greet(me + 1))

    def hop(payload, kind, which):
        column = (col + 2) % COLS if kind == CORE_FAR else col
        return remote(payload, kind, which, column)

    def landing(payload, kind, which):
        beside = col + 1 - 2 * (col % 2)
        column = {DOWN: col, ACROSS: (col + 2) % COLS, CORE: beside, CORE_FAR: (beside + 2) % COLS}[kind]
        return remote(payload, kind, which, column)

    def remote(payload, kind, which, column):
        here = pl.ds(pl.multiple_of((which * COLS + column) * rows, rows), rows)
        ref = places.at[here] if payload == ITERS else blocks.at[payload, here]
        target = {DOWN: me + COLS, ACROSS: across, CORE: other, CORE_FAR: other}[kind]
        return pltpu.make_async_remote_copy(
            src_ref=ref,
            dst_ref=ref,
            send_sem=send_sem.at[payload, kind, which],
            recv_sem=recv_sem.at[payload, kind, which],
            device_id={"seq": target},
            device_id_type=pl.DeviceIdType.MESH,
        )

    def send_on(payload, which):
        pl.when(row < line - 1)(lambda: hop(payload, DOWN, which).start())
        hop(payload, ACROSS, which).start()
        hop(payload, CORE, which).start()

    def tail_copy(step):
        return pltpu.make_async_remote_copy(
            src_ref=tail_src.at[step],
            dst_ref=tail_dst.at[step],
            send_sem=tail_send.at[step],
            recv_sem=tail_recv.at[step],
            device_id={"seq": me + 1},
            device_id_type=pl.DeviceIdType.MESH,
        )

    current[...] = latent[...]
    place_load.wait()
    pl.semaphore_wait(
        barrier,
        3
        + (row > 0).astype(jnp.int32)
        + (row < line - 1).astype(jnp.int32)
        + (me > 0).astype(jnp.int32)
        + (me < n - 1).astype(jnp.int32),
    )

    lane = lax.broadcasted_iota(jnp.int32, (1, pair), 1)
    low = lane < head_dim

    for step in range(ITERS):
        payloads = (ITERS, 0) if step == 0 else (step,)
        value = current[...]
        tail_src[step] = value[rows - TAIL :].astype(BF16)
        pl.when(me < n - 1)(lambda: tail_copy(step).start())
        if step == 0:
            send_on(ITERS, row)
        turned = pltpu.roll(value, 1, 0)
        pl.when(me > 0)(lambda: tail_copy(step).wait_recv())

        @pl.when(me == 0)
        def _():
            tail_dst[step] = jnp.zeros_like(tail_dst[step])

        before = tail_dst[step].astype(F32)[TAIL - 1 :]
        first = lax.broadcasted_iota(jnp.int32, (rows, 1), 0) == 0
        shifted = jnp.where(first, before, turned).astype(BF16)
        blocks[step, own_rows] = shifted
        send_on(step, row)

        if step == 0:
            for load in loads[:4]:
                load.wait()
        hidden_in = dot(shifted, in_w[...]) + places[own_rows].astype(F32)
        normed = rms_norm(hidden_in, gain_attn[...]).astype(BF16)
        query = dot(normed, q_w[...]).astype(BF16).astype(F32) * head_dim ** (-0.5)
        for p in range(pairs):
            both = query[:, p * pair : (p + 1) * pair]
            queries[p, :rows] = jnp.where(low, both, 0.0).astype(BF16)
            queries[p, rows:] = jnp.where(low, 0.0, both).astype(BF16)

        def exchange(which):
            for payload in payloads:
                landing(payload, ACROSS, which).wait_recv()
                hop(payload, CORE_FAR, which).start()

            @pl.when(which > 0)
            def _():
                for payload in payloads:
                    landing(payload, DOWN, which - 1).wait_recv()
                    send_on(payload, which - 1)

            for payload in payloads:
                landing(payload, CORE, which).wait_recv()
                landing(payload, CORE_FAR, which).wait_recv()

        def attend(which, own):
            span = COLS * rows
            here = pl.ds(pl.multiple_of(which * span, span), span)
            hidden = dot(blocks[step, here], in_w[...]) + places[here].astype(F32)
            normed = rms_norm(hidden, gain_attn[...]).astype(BF16)
            keys = dot(normed, k_w[...]).astype(BF16)
            values = dot(normed, v_w[...]).astype(BF16)
            if own:
                query_pos = lax.broadcasted_iota(jnp.int32, (2 * rows, span), 0) % rows + col * rows
                key_pos = lax.broadcasted_iota(jnp.int32, (2 * rows, span), 1)
                causal = key_pos <= query_pos
            for p in range(pairs):
                columns = slice(p * pair, (p + 1) * pair)
                scores = dot_nt(queries[p], keys[:, columns])
                if own:
                    scores = jnp.where(causal, scores, -1e30)
                highest = jnp.max(scores, axis=1, keepdims=True)
                if not own:
                    old = top[p]
                    highest = jnp.maximum(old, highest)
                weights = jnp.exp(scores - highest)
                sums = jnp.sum(weights, axis=1, keepdims=True)
                product = dot(weights.astype(BF16), values[:, columns])
                if own:
                    total[p] = sums
                    acc[p] = product
                else:
                    shrink = jnp.exp(old - highest)
                    total[p] = total[p] * shrink + sums
                    acc[p] = acc[p] * shrink + product
                top[p] = highest

        exchange(row)
        attend(row, True)

        @pl.loop(0, row)
        def _(i):
            which = row - 1 - i
            exchange(which)
            attend(which, False)

        parts = []
        for p in range(pairs):
            result = acc[p] / total[p]
            parts.append(jnp.where(low, result[:rows], result[rows:]).astype(BF16))
        attended = jnp.concatenate(parts, axis=1)
        if step == 0:
            for load in loads[4:]:
                load.wait()
        hidden_mid = hidden_in + dot(attended, mix_w[...])
        normed_mlp = rms_norm(hidden_mid, gain_mlp[...]).astype(BF16)
        activated = jax.nn.gelu(dot(normed_mlp, up_w[...])).astype(BF16)
        hidden_out = hidden_mid + dot(activated, down_w[...])
        normed_out = rms_norm(hidden_out, gain_out[...]).astype(BF16)
        statistics = dot(normed_out, out_w[...])
        mean_shift = statistics[:, :patch]
        log_scale = pltpu.roll(statistics, patch, 1)[:, :patch]
        current[...] = latent[...] * jnp.exp(log_scale) + mean_shift

    flip_src[...] = current[...].astype(BF16)
    flip = pltpu.make_async_remote_copy(
        src_ref=flip_src,
        dst_ref=flip_dst,
        send_sem=flip_send,
        recv_sem=flip_recv,
        device_id={"seq": mirror},
        device_id_type=pl.DeviceIdType.MESH,
    )
    flip.start()

    for step in range(ITERS):
        pl.when(me < n - 1)(lambda: tail_copy(step).wait_send())

    @pl.loop(0, row + 1)
    def _(which):
        for payload in range(ITERS + 1):
            pl.when(row < line - 1)(lambda: hop(payload, DOWN, which).wait_send())
            for kind in (ACROSS, CORE, CORE_FAR):
                hop(payload, kind, which).wait_send()

    flip.wait()
    out[...] = flip_dst[...].astype(F32)


def per_device(
    latent_noise,
    position,
    in_weight,
    gain_attn,
    query_weight,
    key_weight,
    value_weight,
    mix_weight,
    gain_mlp,
    up_weight,
    down_weight,
    gain_out,
    out_weight,
):
    n = lax.axis_size("seq")
    rows, patch = latent_noise.shape
    model = position.shape[1]
    pair = 2 * query_weight.shape[1] // HEADS
    pairs = HEADS // 2
    weights = (
        in_weight,
        query_weight,
        key_weight,
        value_weight,
        mix_weight,
        up_weight,
        down_weight,
        out_weight,
    )
    in_vmem = pl.BlockSpec(memory_space=pltpu.VMEM)
    anywhere = pl.BlockSpec(memory_space=pl.ANY)
    line = n // COLS
    dma = pltpu.SemaphoreType.DMA
    result = pl.pallas_call(
        functools.partial(kernel, n),
        out_shape=jax.ShapeDtypeStruct((rows, patch), F32),
        in_specs=[in_vmem] * 4 + [anywhere] * 9,
        out_specs=in_vmem,
        scratch_shapes=[pltpu.VMEM(w.shape, w.dtype) for w in weights]
        + [
            pltpu.VMEM((ITERS, n * rows, patch), BF16),
            pltpu.VMEM((n * rows, model), BF16),
            pltpu.VMEM((ITERS, TAIL, patch), BF16),
            pltpu.VMEM((ITERS, TAIL, patch), BF16),
            pltpu.VMEM((pairs, 2 * rows, pair), BF16),
            pltpu.VMEM((pairs, 2 * rows, 1), F32),
            pltpu.VMEM((pairs, 2 * rows, 1), F32),
            pltpu.VMEM((pairs, 2 * rows, pair), F32),
            pltpu.VMEM((rows, patch), F32),
            pltpu.VMEM((rows, patch), BF16),
            pltpu.VMEM((rows, patch), BF16),
            dma((len(weights) + 1,)),
            dma((ITERS + 1, 4, line)),
            dma((ITERS + 1, 4, line)),
            dma((ITERS,)),
            dma((ITERS,)),
            dma,
            dma,
        ],
        compiler_params=pltpu.CompilerParams(
            collective_id=0, has_side_effects=True, vmem_limit_bytes=56 * 2**20
        ),
    )(
        latent_noise,
        gain_attn.reshape(1, model),
        gain_mlp.reshape(1, model),
        gain_out.reshape(1, model),
        position,
        *weights,
    )
    return result[::-1]


def solution(mesh):
    in_specs = (P(("groups", "seq"), None), P("seq", None)) + (P(),) * 11
    out_specs = P(("groups", "seq"), None)
    return jax.shard_map(
        per_device, mesh=mesh, in_specs=in_specs, out_specs=out_specs, check_vma=False
    )
```

time: 243 us -> 75.7 us (0.31)
  waiting for transfers between devices: 154 us -> 0 us
  Pallas kernels: 0 us -> 67.6 us
  matrix products: 39.6 us -> 0 us
  between operations: 13.4 us -> 0.01 us
  local copies, waits for them, and re-layouts: 20 us -> 7.05 us
  starting transfers between devices: 9.17 us -> 0 us
  other arithmetic: 4.6 us -> 0 us
    all_gather x4 -> x0, waiting for transfers between devices: 137 us -> none  [the longest x2 75 us: attend_rows(): key_piece = lax.all_gather(key_rows, 'seq', axis=0, tiled=True)]
    pallas_call x0 -> x1, Pallas kernels: none -> 67.6 us  [per_device(): pl.pallas_call(functools.partial(kernel, n), out_shape=jax.ShapeDtypeStru...]
    dot_general x18 -> x0, matrix products: 39.6 us -> none  [the longest x2 9.45 us: attend_rows(): jnp.einsum('hqk,khd->hqd', weights.astype(jnp.bfloat16), value_heads, pre...]
    ppermute x6 -> x0, waiting for transfers between devices: 16.5 us -> none  [the longest x4 15.5 us: swapped(): return lax.ppermute(value, axis, pairs)]
    all_gather x4 -> x0, local copies, waits for them, and re-layouts: 10.6 us -> none  [the longest x2 5.31 us: attend_rows(): key_piece = lax.all_gather(key_rows, 'seq', axis=0, tiled=True)]
    ppermute x6 -> x0, starting transfers between devices: 8.87 us -> none  [the longest x2 6.91 us: shifted_2(): lax.ppermute(value, axis, [(source, source + steps) for source in range(l...]
    unnamed x19 -> x1, local copies, waits for them, and re-layouts: 6.29 us -> 1.63 us
    reshape x0 -> x3, local copies, waits for them, and re-layouts: none -> 3.8 us  [the longest x1 1.27 us: per_device(): gain_out.reshape(1, model)]
  transfers between devices with their start and end apart: 10 -> 0, of which waited for: 10 -> 0; matrix products, arithmetic and copies ran while one was open for 10% -> 0% of each run, Pallas kernels for 0% -> 0%
where the time goes in v1:
time: 75.7 us; the launch traced here: 74.6 us
  Pallas kernels  67.6 us (89%)
  local copies, waits for them, and re-layouts  7.05 us (9%)
    pallas_call x1, Pallas kernels, per_device(): pl.pallas_call(functools.partial(kernel, n), out_shape=jax.ShapeDtypeStru...  67.6 us
    unnamed x1, local copies, waits for them, and re-layouts  1.63 us
    rev x2, local copies, waits for them, and re-layouts, per_device(): return result[::-1]  1.63 us

profile of v1, /device:TPU:1, one launch (start us, length us, event | category | flops | bytes accessed | tf_op | source)
XLA Modules:
  0.0 74.6 jit_solution(5924579422863999236)
XLA Ops:
  0.0 1.3 %reshape.9.gain_attn = f32[1,768]{1,0:T(1,128)} reshape(f32[768]{0:T(1024)} %param.16) | data formatting | bytes 6144 | tf_op jit(solution)/shard_map/reshape | solution.py:345
  1.3 1.3 %reshape.10.gain_mlp = f32[1,768]{1,0:T(1,128)} reshape(f32[768]{0:T(1024)} %param.21) | data formatting | bytes 6144 | tf_op jit(solution)/shard_map/reshape | solution.py:346
  2.5 1.3 %reshape.11.gain_out = f32[1,768]{1,0:T(1,128)} reshape(f32[768]{0:T(1024)} %param.24) | data formatting | bytes 6144 | tf_op jit(solution)/shard_map/reshape | solution.py:347
  3.8 1.6 %copy.14.latent = f32[128,192]{1,0:T(8,128)} copy(f32[128,192]{0,1:T(8,128)} %param.13) | data formatting | bytes 196608 | tf_op args[0]
  5.4 67.6 %shard_map.127 = f32[128,192]{1,0:T(8,128)} custom-call(f32[128,192]{1,0:T(8,128)} %copy.14.latent, f32[1,768]{1,0:T(1,128)} %reshape.9.gain_attn, f32[1,768]{1,0:T(1,128)} %reshape.10.gain_mlp, f32[1,768]{1,0:T(1,128)} %reshape.11.gain_out, bf16[128,768]{1,0:T(8,128)(2,1)} %position.1, bf16[192,768]{1,0:T(8,128)(2,1)} %refs_0_.1, bf16[768,384]{1,0:T(8,128)(2,1)} %refs_1_.1, ...), custom_call_target="tpu_custom_call" | custom-call | tf_op jit(solution)/shard_map/pallas_call | solution.py:314
  73.0 0.9 %rev.3 = f32[128,192]{1,0:T(8,128)S(1)} reverse(f32[128,192]{1,0:T(8,128)} %shard_map.127), dimensions={0} | reverse | bytes 196608 | tf_op jit(solution)/shard_map/rev | solution.py:351
  73.9 0.7 copy.15

commit v2 on v1

--- a/solution.py
+++ b/solution.py
@@ -25,7 +25,7 @@
 
 def rms_norm(values, gain):
     scale = lax.rsqrt(jnp.mean(values * values, axis=-1, keepdims=True) + 1e-06)
-    return values * scale * gain
+    return values * scale * gain.reshape(1, -1)
 
 
 def kernel(
@@ -50,6 +50,7 @@
         top,
         total,
         acc,
+        noise,
         current,
         flip_src,
         flip_dst,
@@ -61,7 +62,7 @@
         flip_send,
         flip_recv,
     ) = scratch[8:]
-    rows, patch = latent.shape
+    patch, rows = latent.shape
     width = q_w.shape[1]
     head_dim = width // HEADS
     pair = 2 * head_dim
@@ -133,7 +134,8 @@
             device_id_type=pl.DeviceIdType.MESH,
         )
 
-    current[...] = latent[...]
+    noise[...] = latent[...].T
+    current[...] = noise[...]
     place_load.wait()
     pl.semaphore_wait(
         barrier,
@@ -178,17 +180,17 @@
             queries[p, :rows] = jnp.where(low, both, 0.0).astype(BF16)
             queries[p, rows:] = jnp.where(low, 0.0, both).astype(BF16)
 
-        def exchange(which):
+        def take(which):
+            for payload in payloads:
+                landing(payload, DOWN, which).wait_recv()
+                send_on(payload, which)
+
+        def pass_far(which):
             for payload in payloads:
                 landing(payload, ACROSS, which).wait_recv()
                 hop(payload, CORE_FAR, which).start()
 
-            @pl.when(which > 0)
-            def _():
-                for payload in payloads:
-                    landing(payload, DOWN, which - 1).wait_recv()
-                    send_on(payload, which - 1)
-
+        def gather(which):
             for payload in payloads:
                 landing(payload, CORE, which).wait_recv()
                 landing(payload, CORE_FAR, which).wait_recv()
@@ -200,6 +202,7 @@
             normed = rms_norm(hidden, gain_attn[...]).astype(BF16)
             keys = dot(normed, k_w[...]).astype(BF16)
             values = dot(normed, v_w[...]).astype(BF16)
+            pl.when(which > 0)(lambda: pass_far(which - 1))
             if own:
                 query_pos = lax.broadcasted_iota(jnp.int32, (2 * rows, span), 0) % rows + col * rows
                 key_pos = lax.broadcasted_iota(jnp.int32, (2 * rows, span), 1)
@@ -225,13 +228,16 @@
                     acc[p] = acc[p] * shrink + product
                 top[p] = highest
 
-        exchange(row)
+        pass_far(row)
+        pl.when(row > 0)(lambda: take(row - 1))
+        gather(row)
         attend(row, True)
 
         @pl.loop(0, row)
         def _(i):
             which = row - 1 - i
-            exchange(which)
+            pl.when(which > 0)(lambda: take(which - 1))
+            gather(which)
             attend(which, False)
 
         parts = []
@@ -250,7 +256,7 @@
         statistics = dot(normed_out, out_w[...])
         mean_shift = statistics[:, :patch]
         log_scale = pltpu.roll(statistics, patch, 1)[:, :patch]
-        current[...] = latent[...] * jnp.exp(log_scale) + mean_shift
+        current[...] = noise[...] * jnp.exp(log_scale) + mean_shift
 
     flip_src[...] = current[...].astype(BF16)
     flip = pltpu.make_async_remote_copy(
@@ -274,7 +280,12 @@
                 hop(payload, kind, which).wait_send()
 
     flip.wait()
-    out[...] = flip_dst[...].astype(F32)
+    from_row = lax.broadcasted_iota(jnp.int32, (rows, rows), 0)
+    to_row = lax.broadcasted_iota(jnp.int32, (rows, rows), 1)
+    turn = jnp.where(from_row + to_row == rows - 1, 1.0, 0.0).astype(BF16)
+    out[...] = lax.dot_general(
+        flip_dst[...], turn, (((0,), (0,)), ((), ())), preferred_element_type=F32
+    )
 
 
 def per_device(
@@ -313,7 +324,7 @@
     dma = pltpu.SemaphoreType.DMA
     result = pl.pallas_call(
         functools.partial(kernel, n),
-        out_shape=jax.ShapeDtypeStruct((rows, patch), F32),
+        out_shape=jax.ShapeDtypeStruct((patch, rows), F32),
         in_specs=[in_vmem] * 4 + [anywhere] * 9,
         out_specs=in_vmem,
         scratch_shapes=[pltpu.VMEM(w.shape, w.dtype) for w in weights]
@@ -326,6 +337,7 @@
             pltpu.VMEM((pairs, 2 * rows, 1), F32),
             pltpu.VMEM((pairs, 2 * rows, 1), F32),
             pltpu.VMEM((pairs, 2 * rows, pair), F32),
+            pltpu.VMEM((rows, patch), F32),
             pltpu.VMEM((rows, patch), F32),
             pltpu.VMEM((rows, patch), BF16),
             pltpu.VMEM((rows, patch), BF16),
@@ -341,14 +353,14 @@
             collective_id=0, has_side_effects=True, vmem_limit_bytes=56 * 2**20
         ),
     )(
-        latent_noise,
-        gain_attn.reshape(1, model),
-        gain_mlp.reshape(1, model),
-        gain_out.reshape(1, model),
+        latent_noise.T,
+        gain_attn,
+        gain_mlp,
+        gain_out,
         position,
         *weights,
     )
-    return result[::-1]
+    return result.T
 
 
 def solution(mesh):

time: 75.7 us -> 74.6 us (0.985); the launches traced: 74.6 us -> 74.4 us
  local copies, waits for them, and re-layouts: 7.05 us -> 1.54 us
  Pallas kernels: 67.6 us -> 72.8 us
    pallas_call x1, Pallas kernels: 67.6 us -> 72.8 us  [per_device(): pl.pallas_call(functools.partial(kernel, n), out_shape=jax.ShapeDtypeStru...]
    reshape x3 -> x0, local copies, waits for them, and re-layouts: 3.8 us -> none  [the longest x1 1.27 us: per_device(): gain_out.reshape(1, model)]
    rev x2 -> x0, local copies, waits for them, and re-layouts: 1.63 us -> none  [per_device(): return result[::-1]]
where the time goes in v2:
time: 74.6 us; the launch traced here: 74.4 us
  Pallas kernels  72.8 us (98%)
  local copies, waits for them, and re-layouts  1.54 us (2%)
    pallas_call x1, Pallas kernels, per_device(): pl.pallas_call(functools.partial(kernel, n), out_shape=jax.ShapeDtypeStru...  72.8 us
    unnamed x1, local copies, waits for them, and re-layouts  1.54 us

profile of v2, /device:TPU:1, one launch (start us, length us, event | category | flops | bytes accessed | tf_op | source)
XLA Modules:
  0.0 74.4 jit_solution(3247798024920512161)
XLA Ops:
  0.0 72.8 %shard_map.127 = f32[192,128]{1,0:T(8,128)} custom-call(f32[192,128]{1,0:T(8,128)} %bitcast.3, f32[768]{0:T(1024)} %gain_attn.1, f32[768]{0:T(1024)} %gain_mlp.1, f32[768]{0:T(1024)} %gain_out.1, bf16[128,768]{1,0:T(8,128)(2,1)} %position.1, bf16[192,768]{1,0:T(8,128)(2,1)} %refs_0_.1, bf16[768,384]{1,0:T(8,128)(2,1)} %refs_1_.1, bf16[768,384]{1,0:T(8,128)(2,1)} %refs_2_.1, ...), custom_call_target="tpu_custom_call" | custom-call | tf_op jit(solution)/shard_map/pallas_call | solution.py:325
  72.8 1.5 %copy.15 = f32[128,192]{0,1:T(8,128)} copy(f32[128,192]{0,1:T(8,128)} %bitcast.2) | data formatting | bytes 196608

commit v3 on v2

--- a/solution.py
+++ b/solution.py
@@ -202,7 +202,8 @@
             normed = rms_norm(hidden, gain_attn[...]).astype(BF16)
             keys = dot(normed, k_w[...]).astype(BF16)
             values = dot(normed, v_w[...]).astype(BF16)
-            pl.when(which > 0)(lambda: pass_far(which - 1))
+            if step > 0:
+                pl.when(which > 0)(lambda: pass_far(which - 1))
             if own:
                 query_pos = lax.broadcasted_iota(jnp.int32, (2 * rows, span), 0) % rows + col * rows
                 key_pos = lax.broadcasted_iota(jnp.int32, (2 * rows, span), 1)
@@ -236,6 +237,8 @@
         @pl.loop(0, row)
         def _(i):
             which = row - 1 - i
+            if step == 0:
+                pass_far(which)
             pl.when(which > 0)(lambda: take(which - 1))
             gather(which)
             attend(which, False)

time: 74.6 us -> 72.2 us (0.968)
  Pallas kernels: 72.8 us -> 70.4 us
    pallas_call x1, Pallas kernels: 72.8 us -> 70.4 us  [per_device(): pl.pallas_call(functools.partial(kernel, n), out_shape=jax.ShapeDtypeStru...]
where the time goes in v3:
time: 72.2 us; the launch traced here: 72 us
  Pallas kernels  70.4 us (98%)
  local copies, waits for them, and re-layouts  1.54 us (2%)
    pallas_call x1, Pallas kernels, per_device(): pl.pallas_call(functools.partial(kernel, n), out_shape=jax.ShapeDtypeStru...  70.4 us
    unnamed x1, local copies, waits for them, and re-layouts  1.54 us

profile of v3, /device:TPU:1, one launch (start us, length us, event | category | flops | bytes accessed | tf_op | source)
XLA Modules:
  0.0 72.0 jit_solution(17692483747544262789)
XLA Ops:
  0.0 70.4 %shard_map.127 = f32[192,128]{1,0:T(8,128)} custom-call(f32[192,128]{1,0:T(8,128)} %bitcast.3, f32[768]{0:T(1024)} %gain_attn.1, f32[768]{0:T(1024)} %gain_mlp.1, f32[768]{0:T(1024)} %gain_out.1, bf16[128,768]{1,0:T(8,128)(2,1)} %position.1, bf16[192,768]{1,0:T(8,128)(2,1)} %refs_0_.1, bf16[768,384]{1,0:T(8,128)(2,1)} %refs_1_.1, bf16[768,384]{1,0:T(8,128)(2,1)} %refs_2_.1, ...), custom_call_target="tpu_custom_call" | custom-call | tf_op jit(solution)/shard_map/pallas_call | solution.py:328
  70.5 1.5 %copy.15 = f32[128,192]{0,1:T(8,128)} copy(f32[128,192]{0,1:T(8,128)} %bitcast.2) | data formatting | bytes 196608

commit v4 on v3

--- a/solution.py
+++ b/solution.py
@@ -10,7 +10,7 @@
 HEADS = 6
 ITERS = 2
 COLS = 4
-DOWN, ACROSS, CORE, CORE_FAR = range(4)
+DOWN, ACROSS, CORE, CORE_FAR, SIDE = range(5)
 TAIL = 16
 F32, BF16 = jnp.float32, jnp.bfloat16
 
@@ -30,6 +30,7 @@
 
 def kernel(
     n,
+    split,
     latent,
     gain_attn,
     gain_mlp,
@@ -73,6 +74,9 @@
     across = row * COLS + (col + 2) % COLS
     other = me + 1 - 2 * (me % 2)
     mirror = n - 1 - me
+    group = lax.axis_index("groups")
+    half = group % 2
+    partner = group + 1 - 2 * half
 
     loads = [
         pltpu.make_async_copy(source, target, load_sem.at[i])
@@ -92,30 +96,38 @@
     greet(across)
     greet(other)
     greet(mirror)
+    if split:
+        pl.semaphore_signal(
+            barrier, inc=1, device_id={"groups": partner}, device_id_type=pl.DeviceIdType.MESH
+        )
     pl.when(row > 0)(lambda: greet(me - COLS))
     pl.when(row < line - 1)(lambda: greet(me + COLS))
     pl.when(me > 0)(lambda: greet(me - 1))
     pl.when(me < n - 1)(lambda: greet(me + 1))
 
     def hop(payload, kind, which):
-        column = (col + 2) % COLS if kind == CORE_FAR else col
-        return remote(payload, kind, which, column)
+        column = (col + 2) % COLS if kind in (CORE_FAR, SIDE) else col
+        return remote(payload, kind, which, column, half)
 
     def landing(payload, kind, which):
         beside = col + 1 - 2 * (col % 2)
-        column = {DOWN: col, ACROSS: (col + 2) % COLS, CORE: beside, CORE_FAR: (beside + 2) % COLS}[kind]
-        return remote(payload, kind, which, column)
-
-    def remote(payload, kind, which, column):
+        column = {DOWN: col, ACROSS: (col + 2) % COLS, SIDE: (col + 2) % COLS, CORE: beside, CORE_FAR: (beside + 2) % COLS}[kind]
+        return remote(payload, kind, which, column, 1 - half if kind == SIDE else half)
+
+    def remote(payload, kind, which, column, share):
         here = pl.ds(pl.multiple_of((which * COLS + column) * rows, rows), rows)
         ref = places.at[here] if payload == ITERS else blocks.at[payload, here]
-        target = {DOWN: me + COLS, ACROSS: across, CORE: other, CORE_FAR: other}[kind]
+        if payload == ITERS and split and kind in (ACROSS, SIDE):
+            part = places.shape[1] // 2
+            ref = places.at[here, pl.ds(pl.multiple_of(share * part, part), part)]
+        target = {DOWN: me + COLS, ACROSS: across, CORE: other, CORE_FAR: other, SIDE: None}[kind]
+        device = {"groups": partner} if kind == SIDE else {"seq": target}
         return pltpu.make_async_remote_copy(
             src_ref=ref,
             dst_ref=ref,
             send_sem=send_sem.at[payload, kind, which],
             recv_sem=recv_sem.at[payload, kind, which],
-            device_id={"seq": target},
+            device_id=device,
             device_id_type=pl.DeviceIdType.MESH,
         )
 
@@ -139,7 +151,7 @@
     place_load.wait()
     pl.semaphore_wait(
         barrier,
-        3
+        (4 if split else 3)
         + (row > 0).astype(jnp.int32)
         + (row < line - 1).astype(jnp.int32)
         + (me > 0).astype(jnp.int32)
@@ -189,6 +201,15 @@
             for payload in payloads:
                 landing(payload, ACROSS, which).wait_recv()
                 hop(payload, CORE_FAR, which).start()
+
+        def sideways(which):
+            landing(ITERS, ACROSS, which).wait_recv()
+            hop(ITERS, SIDE, which).start()
+            landing(0, ACROSS, which).wait_recv()
+            hop(0, CORE_FAR, which).start()
+            pl.when(which > 0)(lambda: take(which - 1))
+            landing(ITERS, SIDE, which).wait_recv()
+            hop(ITERS, CORE_FAR, which).start()
 
         def gather(which):
             for payload in payloads:
@@ -229,17 +250,23 @@
                     acc[p] = acc[p] * shrink + product
                 top[p] = highest
 
-        pass_far(row)
-        pl.when(row > 0)(lambda: take(row - 1))
+        if step == 0 and split:
+            sideways(row)
+        else:
+            pass_far(row)
+            pl.when(row > 0)(lambda: take(row - 1))
         gather(row)
         attend(row, True)
 
         @pl.loop(0, row)
         def _(i):
             which = row - 1 - i
-            if step == 0:
-                pass_far(which)
-            pl.when(which > 0)(lambda: take(which - 1))
+            if step == 0 and split:
+                sideways(which)
+            else:
+                if step == 0:
+                    pass_far(which)
+                pl.when(which > 0)(lambda: take(which - 1))
             gather(which)
             attend(which, False)
 
@@ -281,6 +308,8 @@
             pl.when(row < line - 1)(lambda: hop(payload, DOWN, which).wait_send())
             for kind in (ACROSS, CORE, CORE_FAR):
                 hop(payload, kind, which).wait_send()
+        if split:
+            hop(ITERS, SIDE, which).wait_send()
 
     flip.wait()
     from_row = lax.broadcasted_iota(jnp.int32, (rows, rows), 0)
@@ -326,7 +355,7 @@
     line = n // COLS
     dma = pltpu.SemaphoreType.DMA
     result = pl.pallas_call(
-        functools.partial(kernel, n),
+        functools.partial(kernel, n, lax.axis_size("groups") % 2 == 0),
         out_shape=jax.ShapeDtypeStruct((patch, rows), F32),
         in_specs=[in_vmem] * 4 + [anywhere] * 9,
         out_specs=in_vmem,
@@ -345,8 +374,8 @@
             pltpu.VMEM((rows, patch), BF16),
             pltpu.VMEM((rows, patch), BF16),
             dma((len(weights) + 1,)),
-            dma((ITERS + 1, 4, line)),
-            dma((ITERS + 1, 4, line)),
+            dma((ITERS + 1, 5, line)),
+            dma((ITERS + 1, 5, line)),
             dma((ITERS,)),
             dma((ITERS,)),
             dma,

time: 72.2 us -> 75.3 us (1.043)
  Pallas kernels: 70.4 us -> 73.6 us
    pallas_call x1, Pallas kernels: 70.4 us -> 73.6 us  [per_device(): pl.pallas_call(functools.partial(kernel, n, lax.axis_size('groups') % 2 =...]
where the time goes in v4:
time: 75.3 us; the launch traced here: 75.1 us
  Pallas kernels  73.6 us (98%)
  local copies, waits for them, and re-layouts  1.54 us (2%)
    pallas_call x1, Pallas kernels, per_device(): pl.pallas_call(functools.partial(kernel, n, lax.axis_size('groups') % 2 =...  73.6 us
    unnamed x1, local copies, waits for them, and re-layouts  1.54 us

profile of v4, /device:TPU:1, one launch (start us, length us, event | category | flops | bytes accessed | tf_op | source)
XLA Modules:
  0.0 75.1 jit_solution(10362120951197384952)
XLA Ops:
  0.0 73.6 %shard_map.127 = f32[192,128]{1,0:T(8,128)} custom-call(f32[192,128]{1,0:T(8,128)} %bitcast.3, f32[768]{0:T(1024)} %gain_attn.1, f32[768]{0:T(1024)} %gain_mlp.1, f32[768]{0:T(1024)} %gain_out.1, bf16[128,768]{1,0:T(8,128)(2,1)} %position.1, bf16[192,768]{1,0:T(8,128)(2,1)} %refs_0_.1, bf16[768,384]{1,0:T(8,128)(2,1)} %refs_1_.1, bf16[768,384]{1,0:T(8,128)(2,1)} %refs_2_.1, ...), custom_call_target="tpu_custom_call" | custom-call | tf_op jit(solution)/shard_map/pallas_call | solution.py:357
  73.6 1.5 %copy.15 = f32[128,192]{0,1:T(8,128)} copy(f32[128,192]{0,1:T(8,128)} %bitcast.2) | data formatting | bytes 196608

commit v5 on v3

--- a/solution.py
+++ b/solution.py
@@ -229,17 +229,20 @@
                     acc[p] = acc[p] * shrink + product
                 top[p] = highest
 
-        pass_far(row)
+        if step > 0:
+            pass_far(row)
         pl.when(row > 0)(lambda: take(row - 1))
+        if step == 0:
+            pass_far(row)
         gather(row)
         attend(row, True)
 
         @pl.loop(0, row)
         def _(i):
             which = row - 1 - i
+            pl.when(which > 0)(lambda: take(which - 1))
             if step == 0:
                 pass_far(which)
-            pl.when(which > 0)(lambda: take(which - 1))
             gather(which)
             attend(which, False)
 

time: 72.2 us -> 68.3 us (0.946)
  Pallas kernels: 70.4 us -> 66.6 us
    pallas_call x1, Pallas kernels: 70.4 us -> 66.6 us  [per_device(): pl.pallas_call(functools.partial(kernel, n), out_shape=jax.ShapeDtypeStru...]
where the time goes in v5:
time: 68.3 us; the launch traced here: 68.2 us
  Pallas kernels  66.6 us (98%)
  local copies, waits for them, and re-layouts  1.54 us (2%)
    pallas_call x1, Pallas kernels, per_device(): pl.pallas_call(functools.partial(kernel, n), out_shape=jax.ShapeDtypeStru...  66.6 us
    unnamed x1, local copies, waits for them, and re-layouts  1.54 us

profile of v5, /device:TPU:1, one launch (start us, length us, event | category | flops | bytes accessed | tf_op | source)
XLA Modules:
  0.0 68.2 jit_solution(7841435926932835557)
XLA Ops:
  0.0 66.6 %shard_map.127 = f32[192,128]{1,0:T(8,128)} custom-call(f32[192,128]{1,0:T(8,128)} %bitcast.3, f32[768]{0:T(1024)} %gain_attn.1, f32[768]{0:T(1024)} %gain_mlp.1, f32[768]{0:T(1024)} %gain_out.1, bf16[128,768]{1,0:T(8,128)(2,1)} %position.1, bf16[192,768]{1,0:T(8,128)(2,1)} %refs_0_.1, bf16[768,384]{1,0:T(8,128)(2,1)} %refs_1_.1, bf16[768,384]{1,0:T(8,128)(2,1)} %refs_2_.1, ...), custom_call_target="tpu_custom_call" | custom-call | tf_op jit(solution)/shard_map/pallas_call | solution.py:331
  66.6 1.5 %copy.15 = f32[128,192]{0,1:T(8,128)} copy(f32[128,192]{0,1:T(8,128)} %bitcast.2) | data formatting | bytes 196608
